TPU v7x, 32 devices: a whole 2x2x4 slice. The times are simulated.
32 devices in a mesh: row: 4 (over z), col: 8 (over y, x, core).
Axes of the slice: x: 2, y: 2, z: 4, core: 2. Of those that a mesh axis runs over, the one named last changes fastest.
Arguments:
- front: float32 [62464, 1024], P('row', 'col')
- child_update: bfloat16 [62464, 1024], P('row', 'col'), may hold values from -6 to 6
- child_rows: int32 [4, 244], replicated, may hold values from 8 to 487, as said below
Outputs:
- factor: float32 [62464, 1024], P('row', 'col')
Inputs may be any that keep to these rules, and one draw needn't show every extreme that they name: `child_rows`: each row names 244 distinct parent block rows, none below 8. Block row b of child c lies on row group (c // 2) * 2 + b // 122; the 122 block rows of one row group go to the parent row groups (each owning 122 consecutive block rows) in turn, from a drawn first one, so at most 31 of them reach one parent row group.
All inputs are finite; a program needn't handle non-finite values.
Results may differ from a plain program's by a relative error of at most 0.0017.
Values may be sent and summed in bfloat16 or wider, within the bound.
A program may use at most 128 MiB of HBM per device.

v0:
```python
import jax
import jax.numpy as jnp
from jax import lax
from jax.sharding import PartitionSpec as P

STEPS = 3


def from_root(block, axis, owner):
    block = jnp.where(lax.axis_index(axis) == owner, block, jnp.zeros_like(block))
    return lax.psum(block, axis)


def on_device(front, child_update, child_rows):
    block_cols = front.shape[1]
    local_rows = front.shape[0]
    row_blocks = local_rows // block_cols
    row_count = lax.axis_size("row")
    col_count = lax.axis_size("col")
    row_here = lax.axis_index("row")
    col_here = lax.axis_index("col")
    half_rows = row_count // 2
    col_half = col_here // (col_count // 2)
    child_blocks = child_update.shape[0] // block_cols
    capacity = (child_blocks + row_count - 1) // row_count
    group_ids = jnp.arange(row_count, dtype=jnp.int32)
    source_child = 2 * (group_ids // half_rows) + col_half
    source_first = group_ids % half_rows * child_blocks
    block_ids = child_rows[
        source_child[:, None],
        source_first[:, None] + jnp.arange(child_blocks, dtype=jnp.int32)[None, :],
    ]
    targets = block_ids // row_blocks
    one_hot = (targets[:, :, None] == group_ids[None, None, :]).astype(jnp.int32)
    ranking = jnp.sum((jnp.cumsum(one_hot, axis=1) - one_hot) * one_hot, axis=2)
    slot_index = targets[row_here] * capacity + ranking[row_here]
    tile_stack = child_update.reshape(child_blocks, block_cols, block_cols)
    outgoing = (
        jnp.zeros((row_count * capacity, block_cols, block_cols), jnp.bfloat16)
        .at[slot_index]
        .set(tile_stack)
    )
    incoming = lax.all_to_all(
        outgoing.reshape(row_count, capacity * block_cols, block_cols),
        "row",
        split_axis=0,
        concat_axis=0,
        tiled=True,
    )
    usable = targets == row_here
    positions = jnp.where(usable, group_ids[:, None] * capacity + ranking, row_count * capacity)
    local_blocks = block_ids % row_blocks
    tile_index = (
        jnp.full((row_count * capacity,), row_blocks, jnp.int32)
        .at[positions.reshape(-1)]
        .set(local_blocks.reshape(-1), mode="drop")
    )
    gathered_tiles = incoming.reshape(row_count * capacity, block_cols, block_cols).astype(
        jnp.float32
    )
    contribution = (
        jnp.zeros((row_blocks, block_cols, block_cols), jnp.float32)
        .at[tile_index]
        .add(gathered_tiles, mode="drop")
        .reshape(local_rows, block_cols)
    )
    working = front + contribution
    global_rows = row_here * local_rows + jnp.arange(local_rows, dtype=jnp.int32)[:, None]
    identity = jnp.eye(block_cols, dtype=jnp.float32)
    factor = jnp.zeros((local_rows, block_cols), jnp.float32)
    for panel_step in range(STEPS):
        first_col = panel_step * block_cols
        corner = from_root(working[first_col : first_col + block_cols], "row", 0)
        corner = jnp.where(col_here == panel_step, corner, identity)
        symmetric = jnp.tril(corner) + jnp.tril(corner, -1).T
        lower_factor = jnp.linalg.cholesky(symmetric)
        solved = jax.scipy.linalg.solve_triangular(lower_factor, working.T, lower=True).T
        placed = (
            jnp.zeros((local_rows, block_cols), jnp.float32)
            .at[first_col : first_col + block_cols]
            .set(lower_factor)
        )
        panel_cols = jnp.where(
            global_rows < first_col,
            0.0,
            jnp.where(global_rows < first_col + block_cols, placed, solved),
        )
        factor = jnp.where(col_here == panel_step, panel_cols, factor)
        narrow = from_root(panel_cols.astype(jnp.bfloat16), "col", panel_step)
        slab_part = lax.dynamic_slice_in_dim(narrow, col_here * block_cols, block_cols, 0)
        slab_part = from_root(slab_part, "row", 0)
        update = jnp.dot(narrow, slab_part.T, preferred_element_type=jnp.float32)
        working = jnp.where(col_here > panel_step, working - update, working)
    result = jnp.where(col_here < STEPS, factor, working)
    global_cols = col_here * block_cols + jnp.arange(block_cols, dtype=jnp.int32)[None, :]
    return jnp.where(global_rows >= global_cols, result, 0.0)


def solution(mesh):
    in_specs = (P("row", "col"), P("row", "col"), P())
    out_specs = P("row", "col")
    return jax.shard_map(
        on_device, mesh=mesh, in_specs=in_specs, out_specs=out_specs, check_vma=False
    )
```

profile of v0, /device:TPU:29, one launch (start us, length us, event | category | flops | bytes accessed | tf_op | source)
XLA Modules:
  0.0 734.8 jit_solution(2654555920726176944)
XLA Ops:
  6.7 0.5 copy-done
  7.2 6.8 gather_fusion
  14.9 3.0 broadcast_in_dim.85
  17.8 19.1 %scatter_fusion = bf16[124,128,128]{2,1,0:T(8,128)(2,1)} fusion(bf16[124,128,128]{2,1,0:T(8,128)(2,1)} %broadcast_in_dim.85, s32[122]{0:T(128)S(1)} %fusion.46, bf16[122,128,128]{2,1,0:T(8,128)(2,1)} %bitcast.93), kind=kCustom, calls=%fused_computation.2 | custom fusion | bytes 11993576 | tf_op jit(solution)/shard_map/scatter | solution.py:41
  37.0 4.8 all-to-all-start
  42.0 2.9 scatter_custom_fusion
  45.0 84.5 %all-to-all-done = bf16[4,3968,128]{2,1,0:T(8,128)(2,1)} async-done(((bf16[4,3968,128]{2,1,0:T(8,128)(2,1)}), bf16[4,3968,128]{2,1,0:T(8,128)(2,1)}, u32[]{:S(2)}, u32[]{:S(2)}) %all-to-all-start) | async-done | bytes 4063264 | tf_op jit(solution)/shard_map/all_to_all | solution.py:43
  129.5 6.3 convert.1
  135.8 4.3 broadcast_in_dim.81
  140.1 26.2 %scatter_fusion.1 = f32[122,128,128]{2,1,0:T(8,128)} fusion(f32[122,128,128]{2,1,0:T(8,128)} %broadcast_in_dim.81, s32[124]{0:T(128)S(1)} %compare_select_fusion.4, f32[124,128,128]{2,1,0:T(8,128)} %convert.1), kind=kCustom, calls=%fused_computation.3 | custom fusion | flops 2031616 | bytes 24379888 | tf_op jit(solution)/shard_map/scatter-add | solution.py:64
  166.3 6.0 bitcast_add_fusion
  172.3 3.3 copy-done.4
  175.6 0.6 slice_select_fusion.2
  176.5 32.7 %all-reduce.10.cloned.1.call-done = f32[128,128]{1,0:T(8,128)} async-done(((f32[128,128]{1,0:T(8,128)}), f32[128,128]{1,0:T(8,128)}) %all-reduce.10.cloned.1.call-update) | async-done | bytes 65552 | tf_op jit(solution)/shard_map/psum | solution.py:11
  209.5 11.7 %cholesky.59 = f32[128,128]{1,0:T(8,128)S(1)} custom-call(f32[128,128]{1,0:T(8,128)S(1)} %fusion.20), custom_call_target="Cholesky" | custom-call | tf_op jit(solution)/shard_map/jit(cholesky)/cholesky | solution.py:76
  221.3 0.7 compare_reduce_fusion.2
  222.0 0.7 fusion.29
  222.7 9.8 %custom-call.9 = f32[1,128,128]{1,2,0:T(8,128)S(1)} custom-call(f32[1,128,128]{2,1,0:T(8,128)S(1)} %get-tuple-element.47), custom_call_target="InvertDiagBlocksLowerTriangular" | custom-call | tf_op jit(solution)/shard_map/jit(_solve_triangular)/triangular_solve | solution.py:77
  232.5 20.7 %convert_select_fusion.2 = (bf16[15616,128]{1,0:T(8,128)(2,1)}, f32[15616,128]{1,0:T(8,128)}) fusion(pred[]{:T(512)S(6)} %eq.68, f32[15616,128]{1,0:T(8,128)} %copy-done.4, f32[1,128,128]{1,2,0:T(8,128)S(1)} %custom-call.9, f32[128,128]{1,0:T(8,128)S(1)} %get-tuple-element.48, pred[15616]{0:T(1024)(128)(4,1)S(1)} %get-tuple-element.59, ...), kind=kOutput, calls=%fused_computation.27 | convolution fusion | flops 3078225920 | bytes 20150784 | tf_op jit(solution)/shard_map/jit(_solve_triangular)/triangular_solve | solution.py:77
  253.6 81.4 %all-reduce.12.cloned.1.call-done = bf16[15616,128]{1,0:T(8,128)(2,1)} async-done(((bf16[15616,128]{1,0:T(8,128)(2,1)}), bf16[15616,128]{1,0:T(8,128)(2,1)}) %all-reduce.12.cloned.1.call-update) | async-done | bytes 3997712 | tf_op jit(solution)/shard_map/psum | solution.py:11
  335.0 0.8 dynamic-slice_select_fusion.2
  335.7 12.0 %psum.65 = bf16[128,128]{1,0:T(8,128)(2,1)S(1)} all-reduce(bf16[128,128]{1,0:T(8,128)(2,1)S(1)} %dynamic-slice_select_fusion.2), channel_id=1, replica_groups=mesh['row'=4,'col'=8] {'row'}, use_global_device_ids=true, to_apply=%region_9.12 | all-reduce | flops 16384 | bytes 65536 | tf_op jit(solution)/shard_map/psum | solution.py:11
  347.7 5.7 fusion.2
  353.4 3.3 copy-done.3
  356.7 0.6 slice_select_fusion.1
  357.7 35.2 %all-reduce.14.cloned.1.call-done = f32[128,128]{1,0:T(8,128)} async-done(((f32[128,128]{1,0:T(8,128)}), f32[128,128]{1,0:T(8,128)}) %all-reduce.14.cloned.1.call-update) | async-done | bytes 65552 | tf_op jit(solution)/shard_map/psum | solution.py:11
  393.3 11.7 %cholesky.70 = f32[128,128]{1,0:T(8,128)S(1)} custom-call(f32[128,128]{1,0:T(8,128)S(1)} %copy.33), custom_call_target="Cholesky" | custom-call | tf_op jit(solution)/shard_map/jit(cholesky)/cholesky | solution.py:76
  405.1 0.6 compare_reduce_fusion.1
  405.7 0.6 fusion.30
  406.3 9.8 %custom-call.10 = f32[1,128,128]{1,2,0:T(8,128)S(1)} custom-call(f32[1,128,128]{2,1,0:T(8,128)S(1)} %get-tuple-element.45), custom_call_target="InvertDiagBlocksLowerTriangular" | custom-call | tf_op jit(solution)/shard_map/jit(_solve_triangular)/triangular_solve | solution.py:77
  416.1 21.3 %convert_select_fusion.1 = (bf16[15616,128]{1,0:T(8,128)(2,1)}, f32[15616,128]{1,0:T(8,128)}) fusion(pred[]{:T(512)S(6)} %eq.70, f32[15616,128]{1,0:T(8,128)} %copy-done.3, f32[1,128,128]{1,2,0:T(8,128)S(1)} %custom-call.10, f32[128,128]{1,0:T(8,128)S(1)} %get-tuple-element.46, pred[15616]{0:T(1024)(128)(4,1)S(1)} %fusion.34, ...), kind=kOutput, calls=%fused_computation.26 | convolution fusion | flops 3078225920 | bytes 20150784 | tf_op jit(solution)/shard_map/jit(_solve_triangular)/triangular_solve | solution.py:77
  437.4 81.6 %all-reduce.16.cloned.1.call-done = bf16[15616,128]{1,0:T(8,128)(2,1)} async-done(((bf16[15616,128]{1,0:T(8,128)(2,1)}), bf16[15616,128]{1,0:T(8,128)(2,1)}) %all-reduce.16.cloned.1.call-update) | async-done | bytes 3997712 | tf_op jit(solution)/shard_map/psum | solution.py:11
  519.1 0.8 dynamic-slice_select_fusion.1
  519.8 12.0 %psum.68 = bf16[128,128]{1,0:T(8,128)(2,1)S(1)} all-reduce(bf16[128,128]{1,0:T(8,128)(2,1)S(1)} %dynamic-slice_select_fusion.1), channel_id=1, replica_groups=mesh['row'=4,'col'=8] {'row'}, use_global_device_ids=true, to_apply=%region_12.15 | all-reduce | flops 16384 | bytes 65536 | tf_op jit(solution)/shard_map/psum | solution.py:11
  531.8 5.7 fusion.1
  537.5 3.3 copy-done.2
  540.8 0.6 slice_select_fusion
  541.4 0.3 all-reduce.20.cloned.1.call-start
  541.8 35.3 %all-reduce.18.cloned.1.call-done = f32[128,128]{1,0:T(8,128)} async-done(((f32[128,128]{1,0:T(8,128)}), f32[128,128]{1,0:T(8,128)}) %all-reduce.18.cloned.1.call-update) | async-done | bytes 65552 | tf_op jit(solution)/shard_map/psum | solution.py:11
  577.4 11.7 %cholesky.81 = f32[128,128]{1,0:T(8,128)S(1)} custom-call(f32[128,128]{1,0:T(8,128)S(1)} %fusion.16), custom_call_target="Cholesky" | custom-call | tf_op jit(solution)/shard_map/jit(cholesky)/cholesky | solution.py:76
  589.1 0.7 compare_reduce_fusion
  589.8 0.6 select_bitcast_fusion
  590.5 9.8 %custom-call.11 = f32[1,128,128]{1,2,0:T(8,128)S(1)} custom-call(f32[1,128,128]{2,1,0:T(8,128)S(1)} %get-tuple-element.43), custom_call_target="InvertDiagBlocksLowerTriangular" | custom-call | tf_op jit(solution)/shard_map/jit(_solve_triangular)/triangular_solve | solution.py:77
  600.3 21.6 %convert_select_fusion = (bf16[15616,128]{1,0:T(8,128)(2,1)}, f32[15616,128]{1,0:T(8,128)}) fusion(pred[]{:T(512)S(6)} %eq.61, f32[15616,128]{1,0:T(8,128)} %copy-done.2, f32[1,128,128]{1,2,0:T(8,128)S(1)} %custom-call.11, f32[128,128]{1,0:T(8,128)S(1)} %get-tuple-element.44, pred[15616]{0:T(1024)(128)(4,1)S(1)} %fusion.33, pred[15616]{0:T(1024)(128)(4,1)S(1)} %fusion.34), kind=kOutput, calls=%fused_computation.25 | convolution fusion | flops 3078225920 | bytes 20150784 | tf_op jit(solution)/shard_map/jit(_solve_triangular)/triangular_solve | solution.py:77
  621.9 82.4 %all-reduce.20.cloned.1.call-done = bf16[15616,128]{1,0:T(8,128)(2,1)} async-done(((bf16[15616,128]{1,0:T(8,128)(2,1)}), bf16[15616,128]{1,0:T(8,128)(2,1)}) %all-reduce.20.cloned.1.call-update) | async-done | bytes 3997712 | tf_op jit(solution)/shard_map/psum | solution.py:11
  704.3 0.8 dynamic-slice_select_fusion
  705.1 12.0 %psum.71 = bf16[128,128]{1,0:T(8,128)(2,1)S(1)} all-reduce(bf16[128,128]{1,0:T(8,128)(2,1)S(1)} %dynamic-slice_select_fusion), channel_id=1, replica_groups=mesh['row'=4,'col'=8] {'row'}, use_global_device_ids=true, to_apply=%region_15.18 | all-reduce | flops 16384 | bytes 65536 | tf_op jit(solution)/shard_map/psum | solution.py:11
  717.1 10.9 %fusion.10 = f32[15616,128]{1,0:T(8,128)} fusion(f32[15616,128]{1,0:T(8,128)} %copy-done.2, bf16[15616,128]{1,0:T(8,128)(2,1)} %all-reduce.20.cloned.1.call-done, bf16[128,128]{1,0:T(8,128)(2,1)S(1)} %psum.71, f32[15616,128]{1,0:T(8,128)} %get-tuple-element.56, f32[15616,128]{1,0:T(8,128)} %get-tuple-element.54, f32[15616,128]{1,0:T(8,128)} %get-tuple-element.52, ...), kind=kOutput, calls=%fused_computation.20 | convolution fusion | flops 527695872 | bytes 44070404 | tf_op jit(solution)/shard_map/dot_general | solution.py:92
  (63 shorter events, 3.4 us)
Async XLA Ops:
  6.5 0.7 copy-start
  37.0 92.5 %all-to-all-start = ((bf16[4,3968,128]{2,1,0:T(8,128)(2,1)}), bf16[4,3968,128]{2,1,0:T(8,128)(2,1)}, u32[]{:S(2)}, u32[]{:S(2)}) async-start(bf16[4,3968,128]{2,1,0:T(8,128)(2,1)} %bitcast.92), calls=%async_computation | async-start | bytes 8126464 | tf_op jit(solution)/shard_map/all_to_all | solution.py:43
  41.8 167.4 %all-reduce.10.cloned.1.call-start = ((), (), s32[]{:S(2)}) async-start(), calls=%async_computation.1 | async-start | bytes 131072 | tf_op jit(solution)/shard_map/psum | solution.py:11
  172.3 3.3 copy-start.4
  176.2 158.7 %all-reduce.12.cloned.1.call-start = ((), (), s32[]{:S(2)}) async-start(), calls=%async_computation.2 | async-start | bytes 7995392 | tf_op jit(solution)/shard_map/psum | solution.py:11
  253.3 139.7 %all-reduce.14.cloned.1.call-start = ((), (), s32[]{:S(2)}) async-start(), calls=%async_computation.3 | async-start | bytes 131072 | tf_op jit(solution)/shard_map/psum | solution.py:11
  353.4 3.3 copy-start.3
  357.3 161.7 %all-reduce.16.cloned.1.call-start = ((), (), s32[]{:S(2)}) async-start(), calls=%async_computation.4 | async-start | bytes 7995392 | tf_op jit(solution)/shard_map/psum | solution.py:11
  437.4 139.7 %all-reduce.18.cloned.1.call-start = ((), (), s32[]{:S(2)}) async-start(), calls=%async_computation.5 | async-start | bytes 131072 | tf_op jit(solution)/shard_map/psum | solution.py:11
  537.5 3.3 copy-start.2
  541.4 162.9 %all-reduce.20.cloned.1.call-start = ((), (), s32[]{:S(2)}) async-start(), calls=%async_computation.6 | async-start | bytes 7995392 | tf_op jit(solution)/shard_map/psum | solution.py:11
  717.0 10.9 %copy-start.1 = (s32[4,244]{1,0:T(4,128)S(1)}, s32[4,244]{1,0:T(4,128)}, u32[]{:S(2)}) copy-start(s32[4,244]{1,0:T(4,128)} %param.14) | copy-start | bytes 11716
Sparse Core Ops, SparseCore 0:
  176.4 32.7 all-reduce.9
  253.4 81.4 all-reduce.11
  357.4 35.4 all-reduce.13
  437.5 81.5 all-reduce.15
  541.5 35.4 all-reduce.17
  622.0 82.2 all-reduce.19
where the time goes:
time: 747 us; the launch traced here: 735 us
  waiting for transfers between devices  433 us (58%)
  other arithmetic  113 us (15%)
  matrix products  85.8 us (11%)
  local copies, waits for them, and re-layouts  47.5 us (6%)
  blocking collectives  35.9 us (5%)
  between operations  13.9 us (2%)
    psum x6, waiting for transfers between devices, from_root(): return lax.psum(block, axis)  349 us
    all_to_all x1, waiting for transfers between devices, on_device(): lax.all_to_all(outgoing.reshape(row_count, capacity * block_cols, block_c...  84.5 us
    another operation x3, matrix products, on_device(): jax.scipy.linalg.solve_triangular(lower_factor, working.T, lower=True)  63.6 us
    another operation x9, other arithmetic, on_device(): lower_factor = jnp.linalg.cholesky(symmetric)  37.2 us
    psum x3, blocking collectives, from_root(): return lax.psum(block, axis)  35.9 us
    another operation x6, other arithmetic, on_device(): jax.scipy.linalg.solve_triangular(lower_factor, working.T, lower=True)  31.3 us
    scatter-add x1, other arithmetic, on_device(): contribution = jnp.zeros((row_blocks, block_cols, block_cols), jnp.float3...  26.2 us
    dot_general x3, matrix products, on_device(): update = jnp.dot(narrow, slab_part.T, preferred_element_type=jnp.float32)  22.2 us
  transfers between devices with their start and end apart: 7, of which 7 were waited for; matrix products, arithmetic and copies ran while one was open for 0% of the time, Pallas kernels for 0%

commit v1 on v0

v1 whole, which is shorter than its diff:
```python
import functools

import jax
import jax.numpy as jnp
from jax import lax
from jax.experimental import pallas as pl
from jax.experimental.pallas import tpu as pltpu
from jax.sharding import PartitionSpec as P

STEPS = 3
MESH = pl.DeviceIdType.MESH
EXACT = lax.Precision.HIGHEST
F32 = jnp.float32
BF16 = jnp.bfloat16


def dot_t(a, b, precision=None):
    return lax.dot_general(
        a, b, (((1,), (1,)), ((), ())), precision=precision, preferred_element_type=F32
    )


def tables_kernel(groups, blocks, cap, ids_ref, send_ref, take_ref, count_ref):
    me = lax.axis_index("row")
    half = groups // 2
    col_half = lax.axis_index("col") // (lax.axis_size("col") // 2)

    def clear_send(i, _):
        send_ref[i] = 0
        return 0

    def clear_take(i, _):
        take_ref[i] = groups * cap
        return 0

    lax.fori_loop(0, groups * cap, clear_send, 0)
    lax.fori_loop(0, 2 * blocks, clear_take, 0)
    for g in range(groups):
        count_ref[g] = 0
    mine = 2 * (me // half) + col_half
    mine_first = (me % half) * blocks

    def pack(b, _):
        target = lax.div(ids_ref[mine, mine_first + b], jnp.int32(blocks))
        slot = count_ref[target]
        count_ref[target] = slot + 1
        send_ref[target * cap + slot] = b
        return 0

    lax.fori_loop(0, blocks, pack, 0)
    low = me * blocks
    for g in range(groups):
        child = 2 * (g // half) + col_half
        first = (g % half) * blocks

        def take(b, slot):
            local = ids_ref[child, first + b] - low
            here = (local >= 0) & (local < blocks)

            @pl.when(here)
            def _():
                take_ref[(g // half) * blocks + local] = g * cap + slot

            return slot + here.astype(jnp.int32)

        lax.fori_loop(0, blocks, take, jnp.int32(0))


def routes(chips):
    every = (0, 1, 2, 3)
    if chips == 4:
        wide = [
            (0, 1, (1, 2, 3)),
            (0, 2, (0, 2, 3)),
            (2, 3, (0, 2, 3)),
            (3, 1, (0,)),
            (1, 3, (1,)),
            (3, 2, (1,)),
        ]
        return [wide, wide, [(1, 3, every), (3, 2, every)]]
    return [
        [(q, q + 1, every) for q in range(p // 2, chips - 1)] for p in range(STEPS)
    ]


def front_kernel(
    groups, cols, blocks, cap, chunk, front_ref, child_ref, send_ref, take_ref, out_ref,
    outgoing, incoming, narrow, top, square, lower, inverse, facing, my_inverse,
    local_sem, ex_send, ex_recv, top_send, top_recv, fac_send, fac_recv, pan_send, pan_recv,
):
    block = 128
    head = STEPS * block
    row = lax.axis_index("row")
    col = lax.axis_index("col")
    chip = col // 2
    core = col % 2
    chunks = blocks * block // chunk
    per_chunk = (blocks + chunks - 1) // chunks

    barrier = pltpu.get_barrier_semaphore()

    def greet_row(o, _):
        pl.semaphore_signal(
            barrier, inc=1, device_id={"row": (row + o) % groups}, device_id_type=MESH
        )
        return 0

    def greet_col(o, _):
        pl.semaphore_signal(
            barrier, inc=1, device_id={"col": (col + o) % cols}, device_id_type=MESH
        )
        return 0

    lax.fori_loop(1, groups, greet_row, 0)
    lax.fori_loop(1, cols, greet_col, 0)
    load = pltpu.make_async_copy(front_ref, out_ref, local_sem.at[0])
    load.start()

    def pack(o, dest):
        base = (row + o) % groups * cap

        def one(s, _):
            dest(s, child_ref[send_ref[base + s]])
            return 0

        lax.fori_loop(0, cap, one, 0)

    def to_self(s, tile):
        incoming[row * cap + s] = tile

    def exchange(o):
        return pltpu.make_async_remote_copy(
            src_ref=outgoing.at[o - 1],
            dst_ref=incoming.at[pl.ds(row * cap, cap)],
            send_sem=ex_send.at[o - 1],
            recv_sem=ex_recv.at[o - 1],
            device_id={"row": (row + o) % groups},
            device_id_type=MESH,
        )

    def top_copies(p, j):
        return [
            pltpu.make_async_remote_copy(
                src_ref=front_ref.at[pl.ds(0, head)],
                dst_ref=top.at[p, pl.ds(0, head)],
                send_sem=top_send.at[0, j],
                recv_sem=top_recv.at[0, p],
                device_id={"col": j},
                device_id_type=MESH,
            ),
            pltpu.make_async_remote_copy(
                src_ref=front_ref.at[pl.ds(pl.multiple_of(j * block, block), block)],
                dst_ref=top.at[p, pl.ds(head, block)],
                send_sem=top_send.at[1, j],
                recv_sem=top_recv.at[1, p],
                device_id={"col": j},
                device_id_type=MESH,
            ),
        ]

    def top_local(p):
        return [
            pltpu.make_async_copy(
                front_ref.at[pl.ds(0, head)], top.at[p, pl.ds(0, head)], local_sem.at[1]
            ),
            pltpu.make_async_copy(
                front_ref.at[pl.ds(pl.multiple_of(col * block, block), block)],
                top.at[p, pl.ds(head, block)],
                local_sem.at[2],
            ),
        ]

    pl.semaphore_wait(barrier, groups - 1 + cols - 1)
    for p in range(STEPS):

        @pl.when((row == 0) & (col == p))
        def _():
            for copy in top_local(p):
                copy.start()

            def send(o, _):
                for copy in top_copies(p, (col + o) % cols):
                    copy.start()
                return 0

            lax.fori_loop(1, cols, send, 0)

    for o in range(1, groups):

        def to_out(s, tile, o=o):
            outgoing[o - 1, s] = tile

        pack(o, to_out)
        exchange(o).start()
    pack(0, to_self)
    incoming[groups * cap] = jnp.zeros((block, block), BF16)

    def give(o, ref, at):
        return pltpu.make_async_remote_copy(
            src_ref=ref,
            dst_ref=ref,
            send_sem=fac_send.at[at, o - 1],
            recv_sem=fac_recv.at[at],
            device_id={"row": o},
            device_id_type=MESH,
        )

    lane = lax.broadcasted_iota(jnp.int32, (block, block), 1)
    sub = lax.broadcasted_iota(jnp.int32, (block, block), 0)

    @pl.when(row == 0)
    def _():
        for p in range(STEPS):

            @pl.when(col == p)
            def _():
                for copy in top_local(p):
                    copy.wait()

            @pl.when(col != p)
            def _():
                for copy in top_copies(p, col):
                    copy.wait_recv()

        my_inverse[...] = jnp.zeros((block, block), F32)
        for k in range(STEPS):
            here = pl.ds(k * block, block)
            corner = top[k, here]
            square[...] = jnp.where(sub >= lane, corner, corner.T)
            inverse[...] = jnp.where(sub == lane, 1.0, 0.0).astype(F32)

            def eliminate(i, _):
                whole = square[...]
                pivot = square[pl.ds(i, 1), :]
                unit = inverse[pl.ds(i, 1), :]
                diag = jnp.sum(jnp.where(lane[:1] == i, pivot, 0.0), axis=1, keepdims=True)
                root = jnp.sqrt(diag)
                pivot = pivot / root
                unit = unit / root
                column = jnp.sum(jnp.where(lane == i, whole, 0.0), axis=1, keepdims=True) / root
                column = jnp.where(sub[:, :1] > i, column, 0.0)
                square[...] = jnp.where(sub == i, pivot, whole - column * pivot)
                inverse[...] = jnp.where(sub == i, unit, inverse[...] - column * unit)
                return 0

            lax.fori_loop(0, block, eliminate, 0)
            inv = inverse[...]

            @pl.when(col == k)
            def _():
                lower[...] = jnp.where(lane >= sub, square[...], 0.0).T
                my_inverse[...] = inv

            rounded = dot_t(top[k], inv, EXACT).astype(BF16)
            facing[k] = rounded[head:]
            for later in range(k + 1, STEPS):
                top[later] = top[later] - dot_t(
                    rounded, rounded[later * block : (later + 1) * block]
                )

        def hand_on(o, _):
            give(o, facing, 0).start()
            give(o, my_inverse, 1).start()
            return 0

        lax.fori_loop(1, groups, hand_on, 0)

    @pl.when(row != 0)
    def _():
        give(1, facing, 0).wait_recv()
        give(1, my_inverse, 1).wait_recv()

    for o in range(1, groups):
        exchange(o).wait_recv()
    load.wait()

    plan = routes(cols // 2)

    def panel_copy(p, c, edge, to):
        part = narrow.at[p, pl.ds(pl.multiple_of(c * chunk, 16), chunk)]
        return pltpu.make_async_remote_copy(
            src_ref=part,
            dst_ref=part,
            send_sem=pan_send.at[p, edge, c],
            recv_sem=pan_recv.at[p, c],
            device_id={"col": to},
            device_id_type=MESH,
        )

    def for_sends(p, c, action):
        @pl.when(core == p % 2)
        def _():
            number = {}
            for source, to, classes in plan[p]:
                edge = number.get(source, 0)
                number[source] = edge + 1
                wanted = chip == source
                if len(classes) < 4:
                    kind = c % 4
                    wanted &= functools.reduce(
                        lambda a, b: a | b, [kind == x for x in classes]
                    )

                @pl.when(wanted)
                def _():
                    action(panel_copy(p, c, edge, to * 2 + core))

            sibling = chip > p // 2 if p % 2 else chip >= p // 2

            @pl.when(sibling)
            def _():
                action(panel_copy(p, c, 2, col + 1 - 2 * core))

    def send(p, c):
        for_sends(p, c, lambda copy: copy.start())

    def arrived(p, c):
        panel_copy(p, c, 0, 0).wait_recv()

    def assemble(c):
        def one(b, _):
            r = c * per_chunk + b

            @pl.when(r < blocks)
            def _():
                at = pl.ds(pl.multiple_of(r * block, block), block)
                out_ref[at] = (
                    out_ref[at]
                    + incoming[take_ref[r]].astype(F32)
                    + incoming[take_ref[blocks + r]].astype(F32)
                )

            return 0

        lax.fori_loop(0, per_chunk, one, 0)

    def update(c, count):
        at = pl.ds(pl.multiple_of(c * chunk, 16), chunk)
        value = out_ref[at]
        for p in range(count):
            value = value - dot_t(narrow[p, at], facing[p])
        if count < STEPS:
            pass
        return at, value

    def solve(c, p):
        at, value = update(c, p)
        value = dot_t(value, my_inverse[...], EXACT)
        narrow[p, at] = value.astype(BF16)
        out_ref[at] = value
        send(p, c)

    lag = jnp.where(col < 4, 1, 4)

    def step(s, _):
        @pl.when(s < chunks)
        def _():
            assemble(s)

            @pl.when(col == 0)
            def _():
                solve(s, 0)

            @pl.when((core == 0) & (col > 0))
            def _():
                arrived(0, s)
                send(0, s)

            @pl.when(col == 1)
            def _():
                arrived(0, s)
                solve(s, 1)

            @pl.when((core == 1) & (col > 1))
            def _():
                arrived(1, s)
                send(1, s)

        c = s - lag

        @pl.when((c >= 0) & (c < chunks))
        def _():
            @pl.when((core == 0) & (col > 1))
            def _():
                arrived(1, c)

            @pl.when((core == 1) & (col > 1))
            def _():
                arrived(0, c)

            @pl.when(col == 2)
            def _():
                solve(c, 2)

            @pl.when(col > 2)
            def _():
                arrived(2, c)

                @pl.when(core == 0)
                def _():
                    send(2, c)

                at, value = update(c, STEPS)
                out_ref[at] = value

        return 0

    lax.fori_loop(0, chunks + 4, step, 0)

    @pl.when(row == 0)
    def _():
        def clear(i, _):
            at = pl.ds(pl.multiple_of(i * block, block), block)

            @pl.when(i < col)
            def _():
                out_ref[at] = jnp.zeros((block, block), F32)

            @pl.when((i == col) & (col < STEPS))
            def _():
                out_ref[at] = lower[...]

            @pl.when((i == col) & (col >= STEPS))
            def _():
                out_ref[at] = jnp.where(sub >= lane, out_ref[at], 0.0)

            return 0

        lax.fori_loop(0, cols, clear, 0)

    for o in range(1, groups):
        exchange(o).wait_send()

    @pl.when(row == 0)
    def _():
        def gone(o, _):
            give(o, facing, 0).wait_send()
            give(o, my_inverse, 1).wait_send()
            return 0

        lax.fori_loop(1, groups, gone, 0)
        for p in range(STEPS):

            @pl.when(col == p)
            def _():
                def left(o, _):
                    for copy in top_copies(p, (col + o) % cols):
                        copy.wait_send()
                    return 0

                lax.fori_loop(1, cols, left, 0)

    def drain(c, _):
        for p in range(STEPS):

            @pl.when(col >= p)
            def _():
                for_sends(p, c, lambda copy: copy.wait_send())

        return 0

    lax.fori_loop(0, chunks, drain, 0)


def on_device(front, child_update, child_rows):
    rows, block = front.shape
    groups = lax.axis_size("row")
    cols = lax.axis_size("col")
    blocks = rows // block
    cap = (blocks + groups - 1) // groups
    chunk = max(c for c in range(16, 1025, 16) if rows % c == 0)
    chunks = rows // chunk
    send, take = pl.pallas_call(
        functools.partial(tables_kernel, groups, blocks, cap),
        out_shape=(
            jax.ShapeDtypeStruct((groups * cap,), jnp.int32),
            jax.ShapeDtypeStruct((2 * blocks,), jnp.int32),
        ),
        in_specs=[pl.BlockSpec(memory_space=pltpu.SMEM)],
        out_specs=(
            pl.BlockSpec(memory_space=pltpu.SMEM),
            pl.BlockSpec(memory_space=pltpu.SMEM),
        ),
        scratch_shapes=[pltpu.SMEM((groups,), jnp.int32)],
    )(child_rows)
    dma = pltpu.SemaphoreType.DMA
    return pl.pallas_call(
        functools.partial(front_kernel, groups, cols, blocks, cap, chunk),
        out_shape=jax.ShapeDtypeStruct((rows, block), F32),
        in_specs=[
            pl.BlockSpec(memory_space=pl.ANY),
            pl.BlockSpec(memory_space=pltpu.VMEM),
            pl.BlockSpec(memory_space=pltpu.SMEM),
            pl.BlockSpec(memory_space=pltpu.SMEM),
        ],
        out_specs=pl.BlockSpec(memory_space=pltpu.VMEM),
        scratch_shapes=[
            pltpu.VMEM((groups - 1, cap, block, block), BF16),
            pltpu.VMEM((groups * cap + 1, block, block), BF16),
            pltpu.VMEM((STEPS, rows, block), BF16),
            pltpu.VMEM((STEPS, (STEPS + 1) * block, block), F32),
            pltpu.VMEM((block, block), F32),
            pltpu.VMEM((block, block), F32),
            pltpu.VMEM((block, block), F32),
            pltpu.VMEM((STEPS, block, block), BF16),
            pltpu.VMEM((block, block), F32),
            dma((3,)),
            dma((groups - 1,)),
            dma((groups - 1,)),
            dma((2, cols)),
            dma((2, STEPS)),
            dma((2, groups - 1)),
            dma((2,)),
            dma((STEPS, 3, chunks)),
            dma((STEPS, chunks)),
        ],
        compiler_params=pltpu.CompilerParams(
            collective_id=0, has_side_effects=True, vmem_limit_bytes=52 * 2**20
        ),
    )(front, child_update.reshape(blocks, block, block), send, take)


def solution(mesh):
    in_specs = (P("row", "col"), P("row", "col"), P())
    out_specs = P("row", "col")
    return jax.shard_map(
        on_device, mesh=mesh, in_specs=in_specs, out_specs=out_specs, check_vma=False
    )
```

time: 747 us -> 365 us (0.49); the launches traced: 735 us -> 364 us
  waiting for transfers between devices: 433 us -> 0 us
  Pallas kernels: 0 us -> 357 us
  other arithmetic: 113 us -> 0 us
  matrix products: 85.8 us -> 0 us
  local copies, waits for them, and re-layouts: 47.5 us -> 7 us
  blocking collectives: 35.9 us -> 0 us
  between operations: 13.9 us -> 0.03 us
    pallas_call x0 -> x2, Pallas kernels: none -> 357 us  [the longest x1 346 us: on_device(): pl.pallas_call(functools.partial(front_kernel, groups, cols, blocks, cap,...]
    psum x6 -> x0, waiting for transfers between devices: 349 us -> none  [from_root(): return lax.psum(block, axis)]
    all_to_all x1 -> x0, waiting for transfers between devices: 84.5 us -> none  [on_device(): lax.all_to_all(outgoing.reshape(row_count, capacity * block_cols, block_c...]
    another operation x16 -> x0, other arithmetic: 68.8 us -> none  [the longest x9 37.2 us: on_device(): lower_factor = jnp.linalg.cholesky(symmetric)]
    another operation x3 -> x0, matrix products: 63.6 us -> none  [on_device(): jax.scipy.linalg.solve_triangular(lower_factor, working.T, lower=True)]
    psum x3 -> x0, blocking collectives: 35.9 us -> none  [from_root(): return lax.psum(block, axis)]
    scatter-add x1 -> x0, other arithmetic: 26.2 us -> none  [on_device(): contribution = jnp.zeros((row_blocks, block_cols, block_cols), jnp.float3...]
    dot_general x3 -> x0, matrix products: 22.2 us -> none  [on_device(): update = jnp.dot(narrow, slab_part.T, preferred_element_type=jnp.float32)]
  transfers between devices with their start and end apart: 7 -> 0, of which waited for: 7 -> 0; matrix products, arithmetic and copies ran while one was open for 0% -> 0% of each run, Pallas kernels for 0% -> 0%
where the time goes in v1:
time: 365 us; the launch traced here: 364 us
  Pallas kernels  357 us (98%)
  local copies, waits for them, and re-layouts  7 us (2%)
    pallas_call x1, Pallas kernels, on_device(): pl.pallas_call(functools.partial(front_kernel, groups, cols, blocks, cap,...  346 us
    pallas_call x1, Pallas kernels, on_device(): pl.pallas_call(functools.partial(tables_kernel, groups, blocks, cap), out...  11.5 us

profile of v1, /device:TPU:29, one launch (start us, length us, event | category | flops | bytes accessed | tf_op | source)
XLA Modules:
  0.0 364.5 jit_solution(1350815395213016733)
XLA Ops:
  0.0 11.5 %shard_map.37 = (s32[124]{0:T(128)}, s32[244]{0:T(256)}) custom-call(s32[4,244]{1,0:T(4,128)} %ids_ref.1), custom_call_target="tpu_custom_call" | custom-call | tf_op jit(solution)/shard_map/pallas_call | solution.py:473
  11.5 0.0 copy-start
  11.5 0.7 copy-done
  12.2 0.0 copy-start.1
  12.2 0.7 copy-done.1
  12.9 345.9 %shard_map.38 = f32[15616,128]{1,0:T(8,128)} custom-call(f32[15616,128]{1,0:T(8,128)} %front_ref.1, bf16[122,128,128]{2,1,0:T(8,128)(2,1)} %bitcast.1, s32[124]{0:T(128)S(1)} %copy-done.1, s32[244]{0:T(256)S(1)} %copy-done), custom_call_target="tpu_custom_call" | custom-call | tf_op jit(solution)/shard_map/pallas_call | solution.py:487
  358.8 5.7 %copy.5 = f32[15616,128]{1,0:T(8,128)} copy(f32[15616,128]{1,0:T(8,128)} %shard_map.38) | data formatting | bytes 15990784
Async XLA Ops:
  11.5 0.7 copy-start
  12.2 0.7 copy-start.1

commit v2 on v1

--- a/solution.py
+++ b/solution.py
@@ -69,14 +69,7 @@
 def routes(chips):
     every = (0, 1, 2, 3)
     if chips == 4:
-        wide = [
-            (0, 1, (1, 2, 3)),
-            (0, 2, (0, 2, 3)),
-            (2, 3, (0, 2, 3)),
-            (3, 1, (0,)),
-            (1, 3, (1,)),
-            (3, 2, (1,)),
-        ]
+        wide = [(0, 1, every), (0, 2, every), (2, 3, (0, 2)), (1, 3, (1, 3))]
         return [wide, wide, [(1, 3, every), (3, 2, every)]]
     return [
         [(q, q + 1, every) for q in range(p // 2, chips - 1)] for p in range(STEPS)
@@ -339,8 +332,6 @@
         value = out_ref[at]
         for p in range(count):
             value = value - dot_t(narrow[p, at], facing[p])
-        if count < STEPS:
-            pass
         return at, value
 
     def solve(c, p):
@@ -350,7 +341,7 @@
         out_ref[at] = value
         send(p, c)
 
-    lag = jnp.where(col < 4, 1, 4)
+    lag = jnp.where(col < 3, 2, jnp.where(col < 4, 4, 5))
 
     def step(s, _):
         @pl.when(s < chunks)
@@ -405,7 +396,7 @@
 
         return 0
 
-    lax.fori_loop(0, chunks + 4, step, 0)
+    lax.fori_loop(0, chunks + 5, step, 0)
 
     @pl.when(row == 0)
     def _():
@@ -468,7 +459,7 @@
     cols = lax.axis_size("col")
     blocks = rows // block
     cap = (blocks + groups - 1) // groups
-    chunk = max(c for c in range(16, 1025, 16) if rows % c == 0)
+    chunk = max(c for c in range(16, 2049, 16) if rows % c == 0)
     chunks = rows // chunk
     send, take = pl.pallas_call(
         functools.partial(tables_kernel, groups, blocks, cap),

time: 365 us -> 261 us (0.72)
  Pallas kernels: 357 us -> 254 us
    pallas_call x1, Pallas kernels: 346 us -> 242 us  [on_device(): pl.pallas_call(functools.partial(front_kernel, groups, cols, blocks, cap,...]
where the time goes in v2:
time: 261 us
  Pallas kernels  254 us (97%)
  local copies, waits for them, and re-layouts  7 us (3%)
    pallas_call x1, Pallas kernels, on_device(): pl.pallas_call(functools.partial(front_kernel, groups, cols, blocks, cap,...  242 us
    pallas_call x1, Pallas kernels, on_device(): pl.pallas_call(functools.partial(tables_kernel, groups, blocks, cap), out...  11.5 us
    unnamed x5, local copies, waits for them, and re-layouts  7 us

profile of v2, /device:TPU:29, one launch (start us, length us, event | category | flops | bytes accessed | tf_op | source)
XLA Modules:
  0.0 260.8 jit_solution(12641211245611374664)
XLA Ops:
  0.0 11.5 %shard_map.37 = (s32[124]{0:T(128)}, s32[244]{0:T(256)}) custom-call(s32[4,244]{1,0:T(4,128)} %ids_ref.1), custom_call_target="tpu_custom_call" | custom-call | tf_op jit(solution)/shard_map/pallas_call | solution.py:464
  11.5 0.0 copy-start
  11.5 0.7 copy-done
  12.2 0.0 copy-start.1
  12.2 0.7 copy-done.1
  12.9 242.3 %shard_map.38 = f32[15616,128]{1,0:T(8,128)} custom-call(f32[15616,128]{1,0:T(8,128)} %front_ref.1, bf16[122,128,128]{2,1,0:T(8,128)(2,1)} %bitcast.1, s32[124]{0:T(128)S(1)} %copy-done.1, s32[244]{0:T(256)S(1)} %copy-done), custom_call_target="tpu_custom_call" | custom-call | tf_op jit(solution)/shard_map/pallas_call | solution.py:478
  255.2 5.7 %copy.5 = f32[15616,128]{1,0:T(8,128)} copy(f32[15616,128]{1,0:T(8,128)} %shard_map.38) | data formatting | bytes 15990784
Async XLA Ops:
  11.5 0.7 copy-start
  12.2 0.7 copy-start.1
